TPU v7x, 256 devices: a whole 4x4x8 slice. The times are simulated.
256 devices in a mesh: cfg: 8 (over x, y_hi), front: 32 (over y_lo, z, core).
Axes of the slice: x: 4, y: 4 (y_hi: 2, y_lo: 2; y = y_hi * 2 + y_lo), z: 8, core: 2. Of those that a mesh axis runs over, the one named last changes fastest.
Arguments:
- parent_tiles: float32 [2048, 256, 256], P(('cfg', 'front')), parts along dimension 0, may hold values from -6 to 6
- parent_mean: float32 [2048, 256], P(('cfg', 'front')), parts along dimension 0, may hold values from -6 to 6
- factor_w: float32 [768, 1024, 256], P(('cfg', 'front')), parts along dimension 0, may hold values from -0.1875 to 0.1875
- diag_inverse: float32 [768, 256, 256], P(('cfg', 'front')), parts along dimension 0, may hold values from -6 to 6
- own_mean: float32 [768, 256], P(('cfg', 'front')), parts along dimension 0, may hold values from -6 to 6
- config_weight: float32 [8], P('cfg'), parts along dimension 0, may hold values from 0.2 to 2
- need_owner: int32 [1536, 1], replicated, may hold values from 0 to 31; in each aligned block of 48 rows (0 to 47, 48 to 95, ...) at most 2 rows name the same one
- need_local: int32 [1536], replicated, may hold values from 0 to 7
Outputs:
- sigma_pj: float32 [768, 1024, 256], P(('cfg', 'front')), parts along dimension 0
- sigma_jj: float32 [768, 256, 256], P(('cfg', 'front')), parts along dimension 0
- weighted_variance: float32 [768, 256], P(('cfg', 'front')), parts along dimension 0
- weighted_mean: float32 [768, 256], P(('cfg', 'front')), parts along dimension 0
There are 8 independent parts, one for each index of `cfg`. A program takes and returns all parts, laid end to end along the dimension named above; an argument that names none is the same for every part. Nothing has to cross between parts.
Inputs may be any that keep to these rules, and one draw needn't show every extreme that they name: `need_owner`: in each aligned block of 48 reads (the children of one index of front) at most 2 reads name one owner; some block reaches 2.
All inputs are finite; a program needn't handle non-finite values.
Results may differ from a plain program's by a relative error of at most 0.000094.
Values sent between devices are 32-bit elements; how exact they have to be, the bound alone decides.
A program may use at most 128 MiB of HBM per device.

v0:
```python
import jax
import jax.numpy as jnp
from jax import lax
from jax.sharding import PartitionSpec as P

highest_precision = lax.Precision.HIGHEST


def shards(
    parent_tiles,
    parent_mean,
    factor_w,
    diag_inverse,
    own_mean,
    config_weight,
    need_owner,
    need_local,
):
    fronts = lax.axis_size("front")
    myself = lax.axis_index("front")
    stored = parent_tiles.shape[0]
    tile_size = parent_tiles.shape[1]
    child_count = factor_w.shape[0]
    own_cols = factor_w.shape[2]
    pattern = factor_w.shape[1] // tile_size
    need_count = child_count * pattern * pattern
    capacity = max(2, need_count // fronts + 1)
    owner_table = need_owner[:, 0].reshape(fronts, need_count)
    local_table = need_local.reshape(fronts, need_count)
    positions = jnp.arange(need_count, dtype=jnp.int32)
    earlier = positions[None, :] < positions[:, None]
    same_owner = owner_table[:, :, None] == owner_table[:, None, :]
    item_rank = jnp.sum(same_owner & earlier[None], axis=2)
    slot_range = jnp.arange(capacity, dtype=jnp.int32)
    outgoing = (owner_table[:, None, :] == myself) & (
        item_rank[:, None, :] == slot_range[None, :, None]
    )
    send_local = jnp.sum(jnp.where(outgoing, local_table[:, None, :], 0), axis=2).reshape(-1)
    send_mask = jnp.any(outgoing, axis=2).reshape(-1).astype(jnp.float32)
    my_owner = lax.dynamic_index_in_dim(owner_table, myself, 0, keepdims=False)
    my_rank = lax.dynamic_index_in_dim(item_rank, myself, 0, keepdims=False)
    my_local = lax.dynamic_index_in_dim(local_table, myself, 0, keepdims=False)
    arrival = my_owner * capacity + my_rank
    pair_index = jnp.arange(child_count * pattern, dtype=jnp.int32)
    diagonal_items = pair_index // pattern * pattern * pattern + pair_index % pattern * (
        pattern + 1
    )
    tile_buffer = (jnp.take(parent_tiles, send_local, axis=0) * send_mask[:, None, None]).reshape(
        fronts, capacity, tile_size, tile_size
    )
    received = lax.all_to_all(tile_buffer, "front", split_axis=0, concat_axis=0, tiled=True)
    item_tiles = jnp.take(
        received.reshape(fronts * capacity, tile_size, tile_size), arrival, axis=0
    )
    item_tiles = item_tiles.reshape(child_count, pattern, pattern, tile_size, tile_size)
    blocks = factor_w.reshape(child_count, pattern, tile_size, own_cols)
    sigma_pj = -jnp.einsum("cabij,cbjk->caik", item_tiles, blocks, precision=highest_precision)
    sigma_pj = sigma_pj.reshape(child_count, pattern * tile_size, own_cols)
    full_mean = lax.all_gather(parent_mean, "front", axis=0, tiled=True)
    parent_piece = jnp.take(full_mean, (my_owner * stored + my_local)[diagonal_items], axis=0)
    parent_piece = parent_piece.reshape(child_count, pattern * tile_size)
    sigma_jj = diag_inverse - jnp.einsum(
        "cpj,cpk->cjk", factor_w, sigma_pj, precision=highest_precision
    )
    variance = jnp.diagonal(sigma_jj, axis1=1, axis2=2)
    mean_value = own_mean - jnp.einsum(
        "cp,cpj->cj", parent_piece, factor_w, precision=highest_precision
    )
    weight = config_weight[0]
    return (sigma_pj, sigma_jj, weight * variance, weight * mean_value)


def solution(mesh):
    return jax.shard_map(
        shards,
        mesh=mesh,
        in_specs=(
            P(("cfg", "front"), None, None),
            P(("cfg", "front"), None),
            P(("cfg", "front"), None, None),
            P(("cfg", "front"), None, None),
            P(("cfg", "front"), None),
            P("cfg"),
            P(),
            P(),
        ),
        out_specs=(
            P(("cfg", "front"), None, None),
            P(("cfg", "front"), None, None),
            P(("cfg", "front"), None),
            P(("cfg", "front"), None),
        ),
        check_vma=False,
    )
```

profile of v0, /device:TPU:1, one launch (start us, length us, event | category | flops | bytes accessed | tf_op | source)
XLA Modules:
  0.0 495.0 jit_solution(10310224583315782656)
XLA Ops:
  0.6 0.0 copy-start
  0.7 0.9 reduce
  1.5 0.1 reshape_squeeze.3
  1.6 0.8 convert_reduce_fusion
  2.5 0.8 broadcast_in_dim.58
  3.2 0.1 select_reduce_fusion
  3.4 0.1 copy.23
  3.5 0.1 fusion.8
  3.6 0.1 reshape.229
  3.7 0.1 copy.22
  3.8 0.1 copy.24
  3.9 10.4 %gather_fusion = f32[64,256,256]{2,1,0:T(8,128)} fusion(f32[8,256,256]{2,1,0:T(8,128)} %param.8, s32[1024]{0:T(1024)S(1)} %pad_clamp_fusion.3), kind=kCustom, calls=%fused_computation | custom fusion | bytes 33554688 | tf_op jit(solution)/shard_map/jit(_take)/gather | solution.py:48
  14.3 11.6 %select_multiply_fusion = f32[32,2,256,256]{3,2,1,0:T(8,128)} fusion(f32[32,2,256,256]{3,2,1,0:T(8,128)} %bitcast.50, f32[32,2]{1,0:T(8,128)S(1)} %copy.24, pred[32,2]{1,0:T(8,128)(4,1)S(1)} %copy.22), kind=kLoop, calls=%fused_computation.5 | loop fusion | flops 8388608 | bytes 33554752 | tf_op jit(solution)/shard_map/mul | solution.py:48
  25.9 0.0 copy-start.3
  25.9 0.0 copy-start.4
  25.9 11.3 %all-to-all-start = ((f32[32,2,256,256]{3,2,1,0:T(8,128)}), f32[32,2,256,256]{3,2,1,0:T(8,128)}, u32[]{:S(2)}, u32[]{:S(2)}) async-start(f32[32,2,256,256]{3,2,1,0:T(8,128)} %select_multiply_fusion), calls=%async_computation | async-start | bytes 33554432 | tf_op jit(solution)/shard_map/all_to_all | solution.py:51
  37.2 0.5 broadcast.284
  37.7 0.7 fusion.23
  38.4 0.1 add.138
  38.5 2.3 copy.26
  41.5 0.7 gather_fusion.3
  42.1 0.1 gather.35
  42.2 0.0 copy-done.3
  42.2 393.0 %all_gather.3 = f32[256,256]{1,0:T(8,128)S(1)} all-gather(f32[8,256]{1,0:T(8,128)S(1)} %copy-done.3), channel_id=1, replica_groups=mesh['cfg'=8,'front'=32] {'front'}, dimensions={0}, use_global_device_ids=true | all-gather | bytes 270336 | tf_op jit(solution)/shard_map/all_gather | solution.py:59
  435.2 0.6 gather_fusion.4
  435.8 0.1 broadcast_bitcast_fusion
  435.9 0.0 copy-done
  436.0 1.6 fusion.9
  437.5 0.0 copy-done.4
  437.5 0.6 fusion.11
  438.1 0.0 all-to-all-done
  438.1 13.6 %gather_fusion.1 = f32[48,256,256]{2,1,0:T(8,128)} fusion(f32[64,256,256]{2,1,0:T(8,128)} %bitcast.2, s32[1024]{0:T(1024)S(1)} %pad_clamp_fusion.2), kind=kCustom, calls=%fused_computation.1 | custom fusion | bytes 25166016 | tf_op jit(solution)/shard_map/jit(_take)/gather | solution.py:52
  451.8 0.0 copy-start.2
  451.8 12.7 %bitcast_negate_fusion = f32[3,4,256,256]{3,2,1,0:T(8,128)S(1)} fusion(f32[3,4,256,256,1]{3,2,1,4,0:T(8,128)S(1)} %bitcast.49, f32[3,4,4,256,256]{4,3,2,1,0:T(8,128)} %bitcast.51, pred[3,4,4]{2,1,0:T(4,128)(4,1)S(1)} %compare_and_fusion), kind=kOutput, calls=%fused_computation.10 | convolution fusion | flops 9667608576 | bytes 18874416 | tf_op jit(solution)/shard_map/cabij,cbjk->caik/dot_general | solution.py:57
  464.5 0.0 copy-start.1
  464.5 1.7 copy-done.1
  466.2 0.0 copy-done.2
  466.2 6.2 %fusion.6 = f32[3,256,256]{1,2,0:T(8,128)} fusion(f32[3,256,256]{1,2,0:T(8,128)S(1)} %copy-done.2, f32[3,1024,256]{2,1,0:T(8,128)S(1)} %bitcast.53, f32[3,1024,256]{2,1,0:T(8,128)S(1)} %copy-done), kind=kOutput, calls=%fused_computation.12 | convolution fusion | flops 2416115712 | bytes 7864320 | tf_op jit(solution)/shard_map/cpj,cpk->cjk/dot_general | solution.py:62
  472.4 17.2 %copy.27 = f32[3,256,256]{0,2,1:T(8,128)} copy(f32[3,256,256]{1,2,0:T(8,128)} %fusion.6) | data formatting | bytes 1572864 | tf_op jit(solution)/shard_map/sub | solution.py:62
  489.7 2.3 copy.28
  491.9 2.3 gather_fusion.2
  494.3 0.7 copy.29
  (19 shorter events, 0.2 us)
Async XLA Ops:
  0.6 435.3 %copy-start = (f32[3,1024,256]{2,1,0:T(8,128)S(1)}, f32[3,1024,256]{2,1,0:T(8,128)}, u32[]{:S(2)}) copy-start(f32[3,1024,256]{2,1,0:T(8,128)} %param.10) | copy-start | bytes 9437188
  25.9 16.3 %copy-start.3 = (f32[8,256]{1,0:T(8,128)S(1)}, f32[8,256]{1,0:T(8,128)}, u32[]{:S(2)}) copy-start(f32[8,256]{1,0:T(8,128)} %param.9) | copy-start | bytes 24580
  25.9 411.6 %copy-start.4 = (f32[3,256]{1,0:T(4,128)S(1)}, f32[3,256]{1,0:T(4,128)}, u32[]{:S(2)}) copy-start(f32[3,256]{1,0:T(4,128)} %param.12) | copy-start | bytes 9220
  25.9 412.2 %all-to-all-start = ((f32[32,2,256,256]{3,2,1,0:T(8,128)}), f32[32,2,256,256]{3,2,1,0:T(8,128)}, u32[]{:S(2)}, u32[]{:S(2)}) async-start(f32[32,2,256,256]{3,2,1,0:T(8,128)} %select_multiply_fusion), calls=%async_computation | async-start | bytes 33554432 | tf_op jit(solution)/shard_map/all_to_all | solution.py:51
  451.8 14.4 %copy-start.2 = (f32[3,256,256]{1,2,0:T(8,128)S(1)}, f32[3,256,256]{1,2,0:T(8,128)}, u32[]{:S(2)}) copy-start(f32[3,256,256]{1,2,0:T(8,128)} %copy.26) | copy-start | bytes 2359300
  464.5 1.7 copy-start.1
where the time goes:
time: 496 us; the launch traced here: 495 us
  blocking collectives  393 us (79%)
  local copies, waits for them, and re-layouts  53.8 us (11%)
  matrix products  20.5 us (4%)
  other arithmetic  14.9 us (3%)
  starting transfers between devices  11.3 us (2%)
    all_gather x1, blocking collectives, shards(): full_mean = lax.all_gather(parent_mean, 'front', axis=0, tiled=True)  393 us
    sub x1, local copies, waits for them, and re-layouts, shards(): diag_inverse - jnp.einsum('cpj,cpk->cjk', factor_w, sigma_pj, precision=h...  17.2 us
    gather x1, local copies, waits for them, and re-layouts, shards(): jnp.take(received.reshape(fronts * capacity, tile_size, tile_size), arriv...  13.6 us
    dot_general x1, matrix products, shards(): jnp.einsum('cabij,cbjk->caik', item_tiles, blocks, precision=highest_prec...  12.7 us
    mul x1, other arithmetic, shards(): jnp.take(parent_tiles, send_local, axis=0) * send_mask[:, None, None]  11.6 us
    all_to_all x1, starting transfers between devices, shards(): lax.all_to_all(tile_buffer, 'front', split_axis=0, concat_axis=0, tiled=T...  11.3 us
    gather x1, local copies, waits for them, and re-layouts, shards(): jnp.take(parent_tiles, send_local, axis=0) * send_mask[:, None, None]  10.4 us
  transfers between devices with their start and end apart: 1, of which 0 were waited for; matrix products, arithmetic and copies ran while one was open for 1% of the time, Pallas kernels for 0%

commit v1 on v0

--- a/solution.py
+++ b/solution.py
@@ -1,12 +1,462 @@
+import functools
+
 import jax
 import jax.numpy as jnp
 from jax import lax
+from jax.experimental import pallas as pl
+from jax.experimental.pallas import tpu as pltpu
 from jax.sharding import PartitionSpec as P
 
 highest_precision = lax.Precision.HIGHEST
-
-
-def shards(
+MESH = pl.DeviceIdType.MESH
+
+LEVELS = 8
+CHIPS = 16
+STORED = 8
+CHIP_TILES = 16
+SLOTS = 256
+LINKS = 3
+WINDOWS = 26
+POOL = CHIP_TILES + 2 * LINKS * WINDOWS
+RING = 4
+REACH = 5
+NONE = -1.0e6
+
+
+def split_bf16(value):
+    high = value.astype(jnp.bfloat16)
+    return high, (value - high.astype(jnp.float32)).astype(jnp.bfloat16)
+
+
+def dot3(left_high, left_low, right_high, right_low):
+    def dot(left, right):
+        return jnp.dot(left, right, preferred_element_type=jnp.float32)
+
+    return dot(left_high, right_high) + (dot(left_high, right_low) + dot(left_low, right_high))
+
+
+def plan_kernel(slots_ref, out_ref, table_ref, pool_ref):
+    shape = (CHIPS, SLOTS)
+    row = lax.broadcasted_iota(jnp.int32, shape, 0)
+    lane = lax.broadcasted_iota(jnp.int32, shape, 1)
+    chip_y, chip_z = row >> 3, row & 7
+    owner_y, owner_z, owner_core = lane >> 7, (lane >> 4) & 7, (lane >> 3) & 1
+    slots = slots_ref[...]
+    need = jnp.zeros(shape, jnp.float32)
+    for item in range(slots.shape[1]):
+        need = jnp.where(slots[:, item : item + 1] == lane, 1.0, need)
+
+    def swapped(value):
+        return jnp.concatenate([value[LEVELS:], value[:LEVELS]], axis=0)
+
+    def turned(value, by):
+        return jnp.concatenate(
+            [pltpu.roll(value[:LEVELS], by, 0), pltpu.roll(value[LEVELS:], by, 0)], axis=0
+        )
+
+    def most(value):
+        return jnp.max(value, axis=0, keepdims=True)
+
+    other_need = swapped(need)
+    level_need = jnp.maximum(need, other_need) > 0.0
+    ahead = ((chip_z - owner_z) & 7).astype(jnp.float32)
+    behind = ((owner_z - chip_z) & 7).astype(jnp.float32)
+    on_owner_line = chip_y == owner_y
+    one_lane = lax.broadcasted_iota(jnp.int32, (1, SLOTS), 1)
+    even = (one_lane & 1) == 0
+    best = jnp.full((1, SLOTS), 1.0e6, jnp.float32)
+    up = jnp.zeros((1, SLOTS), jnp.float32)
+    down = jnp.zeros((1, SLOTS), jnp.float32)
+    for cut in range(LEVELS - 1 - REACH, REACH + 1):
+        cut_up = most(jnp.where(level_need & (ahead <= cut), ahead, 0.0))
+        cut_down = most(jnp.where(level_need & (behind <= LEVELS - 1 - cut), behind, 0.0))
+        cost = (cut_up + cut_down) * 100.0 + jnp.abs(cut_up - cut_down) * 10.0
+        cost = cost + jnp.where((cut_up > cut_down) == even, 1.0, 0.0)
+        better = cost < best
+        best = jnp.where(better, cost, best)
+        up = jnp.where(better, cut_up, up)
+        down = jnp.where(better, cut_down, down)
+    own_count = jnp.sum(jnp.where(on_owner_line & (ahead > 0.0), need, 0.0), axis=0, keepdims=True)
+    other_count = jnp.sum(jnp.where(on_owner_line, 0.0, need), axis=0, keepdims=True)
+    crosses = jnp.where(other_count - own_count - 1.0 > 0.0, 1.0, 0.0)
+    on_line = jnp.where(on_owner_line, 1.0 - crosses, crosses) > 0.0
+    at_owner = on_owner_line & (ahead == 0.0)
+    at_level = ahead == 0.0
+    send_up = on_line & (ahead < up)
+    send_down = on_line & (behind < down)
+    reached = (ahead <= up) | (behind <= down)
+    crossing = at_owner & (crosses > 0.0)
+    send_over = crossing | (
+        on_line & reached & (other_need > 0.0) & jnp.logical_not(at_level & (crosses > 0.0))
+    )
+    end_up = most(jnp.where(on_line & (ahead == up), other_need, 0.0))
+    end_down = most(jnp.where(on_line & (behind == down), other_need, 0.0))
+    longest = jnp.maximum(2.0 * up + end_up, 2.0 * down + end_down)
+    rank_up = 2.0 * (up - ahead) + end_up
+    rank_down = 2.0 * (down - behind) + end_down
+    rank_over = jnp.where(crossing, longest + 2.0, 1.0)
+    key_up = jnp.where(send_up, rank_up * 256.0, NONE)
+    key_down = jnp.where(send_down, rank_down * 256.0, NONE)
+    key_over = jnp.where(send_over, rank_over * 256.0, NONE)
+    held = jnp.where(at_owner, (255 - (lane & 15)).astype(jnp.float32), NONE)
+
+    def window(w, carry):
+        keys, held, coming, table = list(carry[:3]), carry[3], carry[4], carry[5]
+        arrives = []
+        for link in range(LINKS):
+            sent = jnp.full(shape, NONE, jnp.float32)
+            for core in range(2):
+                key = keys[link] + held
+                key = jnp.where((owner_core == core) | (w >= 2), key, NONE)
+                top = jnp.max(key, axis=1, keepdims=True)
+                hit = (key == top) & (top > 0.0)
+                keys[link] = jnp.where(hit, NONE, keys[link])
+                place = CHIP_TILES + link * 2 * WINDOWS + 2 * w + core
+                sent = jnp.where(hit, (255 - place).astype(jnp.float32), sent)
+                found = jnp.where(top > 0.0, 255 - (top.astype(jnp.int32) & 255), 0)
+                table = jnp.where(lane == 6 * w + 2 * link + core, found, table)
+            arrives.append(sent)
+        fresh = jnp.maximum(
+            jnp.maximum(turned(arrives[0], 1), turned(arrives[1], LEVELS - 1)), swapped(arrives[2])
+        )
+        return (*keys, jnp.maximum(held, coming), fresh, table)
+
+    carry = (
+        key_up,
+        key_down,
+        key_over,
+        held,
+        jnp.full(shape, NONE, jnp.float32),
+        jnp.zeros(shape, jnp.int32),
+    )
+    key_up, key_down, key_over, held, coming, table = lax.fori_loop(0, WINDOWS, window, carry)
+    held = jnp.maximum(held, coming)
+    table_ref[...] = table
+    pool_ref[...] = jnp.where(held >= 0.0, 255 - held.astype(jnp.int32), 0)
+    left = jnp.maximum(jnp.maximum(key_up, key_down), key_over)
+    fits = jnp.where(jnp.max(left) > 0.0, 0, 1)
+    chip = lax.axis_index("front") // 2
+    out_ref[...] = jnp.zeros(out_ref.shape, jnp.int32)
+    out_ref[0:1, :] = table_ref[pl.ds(chip, 1), :]
+    out_ref[1:2, :] = pool_ref[pl.ds(chip, 1), :]
+    out_ref[2:3, :] = jnp.full((1, SLOTS), fits, jnp.int32)
+
+
+def exchange_kernel(
+    plan_ref,
+    item_ref,
+    weight_ref,
+    tiles_ref,
+    mean_ref,
+    factor_ref,
+    diag_ref,
+    own_mean_ref,
+    pj_ref,
+    jj_ref,
+    variance_ref,
+    out_mean_ref,
+    pool,
+    land,
+    passed,
+    outgoing,
+    high,
+    low,
+    turned_high,
+    turned_low,
+    stage,
+    jj,
+    means,
+    send_sem,
+    land_sem,
+    pass_send_sem,
+    pass_sem,
+    swap_sem,
+    ring_send_sem,
+    ring_sem,
+    mean_sem,
+    stage_sem,
+    jj_sem,
+    out_sem,
+    credit,
+    pass_credit,
+):
+    cfg, me = lax.axis_index("cfg"), lax.axis_index("front")
+    y, z, core = me // 16, (me // 2) % 8, me % 2
+    children = factor_ref.shape[0]
+
+    def device(to_y, to_z, to_core):
+        return (cfg, to_y * 16 + to_z * 2 + to_core)
+
+    above = device(y, (z + 1) % 8, core)
+    below = device(y, (z + 7) % 8, core)
+    across = device(1 - y, z, core)
+    partner = device(y, z, 1 - core)
+    targets = (above, below, across)
+    sources = (below, above, across)
+
+    def signal(sem, to):
+        pl.semaphore_signal(sem, inc=1, device_id=to, device_id_type=MESH)
+
+    def remote(src, dst, sent, got, to):
+        return pltpu.make_async_remote_copy(
+            src_ref=src,
+            dst_ref=dst,
+            send_sem=sent,
+            recv_sem=got,
+            device_id=to,
+            device_id_type=MESH,
+        )
+
+    def load_stage(child):
+        return pltpu.make_async_copy(factor_ref.at[child], stage, stage_sem)
+
+    jj_load = pltpu.make_async_copy(diag_ref, jj, jj_sem.at[0])
+    load_stage(0).start()
+    jj_load.start()
+    barrier = pltpu.get_barrier_semaphore()
+    for neighbour in (above, below, across, partner):
+        signal(barrier, neighbour)
+    line = y * 2 + core
+    means[line, z] = mean_ref[...]
+    pl.semaphore_wait(barrier, 4)
+
+    own = pl.ds(core * STORED, STORED)
+    swap = remote(tiles_ref, pool.at[own], swap_sem.at[0], swap_sem.at[1], partner)
+
+    def ring(step):
+        block = means.at[line, (z + 8 - step) % 8]
+        return remote(block, block, ring_send_sem.at[step], ring_sem.at[step], above)
+
+    def send(w, link):
+        return remote(
+            outgoing.at[link, w % 2],
+            land.at[link * RING + w % RING],
+            send_sem.at[link, w % 2],
+            land_sem.at[link, w % RING],
+            targets[link],
+        )
+
+    def hand_over(v, link):
+        place = link * RING + v % RING
+        return remote(
+            land.at[place],
+            passed.at[place],
+            pass_send_sem.at[link, v % RING],
+            pass_sem.at[link, v % RING],
+            partner,
+        )
+
+    for w in range(2):
+        for link in range(LINKS):
+            outgoing[link, w] = tiles_ref[plan_ref[0, 6 * w + 2 * link + core] % STORED]
+            send(w, link).start()
+        if w == 0:
+            swap.start()
+            ring(0).start()
+
+    def keep(tile, carry):
+        pool[core * STORED + tile] = tiles_ref[tile]
+        return carry
+
+    lax.fori_loop(0, STORED, keep, 0)
+    swap.wait()
+
+    def take(v):
+        for link in range(LINKS):
+            send(v, link).wait_recv()
+
+            @pl.when(v >= RING)
+            def _():
+                pl.semaphore_wait(pass_credit.at[link], 1)
+
+            hand_over(v, link).start()
+        for link in range(LINKS):
+            place = CHIP_TILES + link * 2 * WINDOWS + 2 * v
+            pool[place + core] = land[link * RING + v % RING]
+        for link in range(LINKS):
+            hand_over(v, link).wait_send()
+
+            @pl.when(v < WINDOWS - RING)
+            def _():
+                signal(credit.at[link], sources[link])
+
+        for link in range(LINKS):
+            hand_over(v, link).wait_recv()
+            place = CHIP_TILES + link * 2 * WINDOWS + 2 * v
+            pool[place + 1 - core] = passed[link * RING + v % RING]
+
+            @pl.when(v < WINDOWS - RING)
+            def _():
+                signal(pass_credit.at[link], partner)
+
+    both = means.at[pl.ds(y * 2, 2)]
+    line_swap = remote(means.at[line], means.at[line], mean_sem.at[0], mean_sem.at[1], partner)
+    mean_swap = remote(both, both, mean_sem.at[2], mean_sem.at[3], across)
+
+    def window(w, carry):
+        take(w - 2)
+        for link in range(LINKS):
+            send(w, link).wait_send()
+            outgoing[link, w % 2] = pool[plan_ref[0, 6 * w + 2 * link + core]]
+
+            @pl.when(w >= RING)
+            def _():
+                pl.semaphore_wait(credit.at[link], 1)
+
+            send(w, link).start()
+
+        @pl.when(w < 9)
+        def _():
+            ring(w - 2).wait()
+
+            @pl.when(w < 8)
+            def _():
+                ring(w - 1).start()
+
+        @pl.when(w == 9)
+        def _():
+            line_swap.start()
+
+        @pl.when(w == 10)
+        def _():
+            line_swap.wait()
+            mean_swap.start()
+
+        @pl.when(w == 11)
+        def _():
+            mean_swap.wait()
+
+        @pl.when((w >= 3) & (w < 3 + children))
+        def _():
+            child = w - 3
+            load_stage(child).wait()
+            for b in range(4):
+                rows = pl.ds(child * 1024 + b * 256, 256)
+                block = stage[b * 256 : (b + 1) * 256, :]
+                high[rows, :], low[rows, :] = split_bf16(block)
+                cols = pl.ds(b * 256, 256)
+                block_t = block.T
+                turned_high[child, :, cols], turned_low[child, :, cols] = split_bf16(block_t)
+
+            @pl.when(child + 1 < children)
+            def _():
+                load_stage(child + 1).start()
+
+        return carry
+
+    lax.fori_loop(2, WINDOWS, window, 0)
+    take(WINDOWS - 2)
+    take(WINDOWS - 1)
+    for w in range(WINDOWS - 2, WINDOWS):
+        for link in range(LINKS):
+            send(w, link).wait_send()
+    jj_load.wait()
+
+    weight = weight_ref[0]
+    rows_at = lax.broadcasted_iota(jnp.int32, (256, 256), 0)
+    cols_at = lax.broadcasted_iota(jnp.int32, (256, 256), 1)
+
+    def pj_out(place):
+        return pltpu.make_async_copy(
+            land.at[place], pj_ref.at[place // 4, pl.ds((place % 4) * 256, 256)], out_sem.at[place]
+        )
+
+    def jj_out(child):
+        return pltpu.make_async_copy(jj.at[child], jj_ref.at[child], jj_sem.at[child])
+
+    def front(child, carry):
+        def pattern_row(a, carry):
+            total = jnp.zeros((256, 256), jnp.float32)
+            for b in range(4):
+                item = plan_ref[1, item_ref[child * 16 + a * 4 + b]]
+                tile_high, tile_low = split_bf16(pool[item])
+                rows = pl.ds(child * 1024 + b * 256, 256)
+                total += dot3(tile_high, tile_low, high[rows, :], low[rows, :])
+            block = -total
+            place = child * 4 + a
+            land[place] = block
+            pj_out(place).start()
+            block_high, block_low = split_bf16(block)
+            cols = pl.ds(pl.multiple_of(a * 256, 256), 256)
+            jj[child] -= dot3(
+                turned_high[child, :, cols], turned_low[child, :, cols], block_high, block_low
+            )
+            return carry
+
+        lax.fori_loop(0, 4, pattern_row, 0)
+        jj_out(child).start()
+        diagonal = jnp.where(rows_at == cols_at, jj[child], 0.0)
+        variance_ref[pl.ds(child, 1), :] = weight * jnp.sum(diagonal, axis=0, keepdims=True)
+        total = jnp.zeros((16, 256), jnp.float32)
+        for a in range(4):
+            slot = item_ref[child * 16 + a * 5]
+            slot_line = slot // 128 * 2 + slot // 8 % 2
+            piece = means[slot_line, slot // 16 % 8, pl.ds(slot % 8, 1), :]
+            piece_high, piece_low = split_bf16(jnp.broadcast_to(piece, (16, 256)))
+            rows = pl.ds(child * 1024 + a * 256, 256)
+            total += dot3(piece_high, piece_low, high[rows, :], low[rows, :])
+        value = own_mean_ref[pl.ds(child, 1), :] - total[0:1]
+        out_mean_ref[pl.ds(child, 1), :] = weight * value
+        return carry
+
+    lax.fori_loop(0, children, front, 0)
+    for child in range(children):
+        for a in range(4):
+            pj_out(child * 4 + a).wait()
+        jj_out(child).wait()
+
+
+def exchange(plan, items, parent_tiles, parent_mean, factor_w, diag_inverse, own_mean, config_weight):
+    tile = parent_tiles.shape[1:]
+    children, depth, width = factor_w.shape
+    vmem = pl.BlockSpec(memory_space=pltpu.VMEM)
+    smem = pl.BlockSpec(memory_space=pltpu.SMEM)
+    anywhere = pl.BlockSpec(memory_space=pl.ANY)
+    dma = pltpu.SemaphoreType.DMA
+    f32, bf16 = jnp.float32, jnp.bfloat16
+    return pl.pallas_call(
+        exchange_kernel,
+        out_shape=(
+            jax.ShapeDtypeStruct(factor_w.shape, f32),
+            jax.ShapeDtypeStruct(diag_inverse.shape, f32),
+            jax.ShapeDtypeStruct(own_mean.shape, f32),
+            jax.ShapeDtypeStruct(own_mean.shape, f32),
+        ),
+        in_specs=[smem, smem, smem, vmem, vmem, anywhere, anywhere, vmem],
+        out_specs=(anywhere, anywhere, vmem, vmem),
+        scratch_shapes=[
+            pltpu.VMEM((POOL, *tile), f32),
+            pltpu.VMEM((LINKS * RING, *tile), f32),
+            pltpu.VMEM((LINKS * RING, *tile), f32),
+            pltpu.VMEM((LINKS, 2, *tile), f32),
+            pltpu.VMEM((children * depth, width), bf16),
+            pltpu.VMEM((children * depth, width), bf16),
+            pltpu.VMEM((children, width, depth), bf16),
+            pltpu.VMEM((children, width, depth), bf16),
+            pltpu.VMEM((depth, width), f32),
+            pltpu.VMEM(diag_inverse.shape, f32),
+            pltpu.VMEM((4, LEVELS, *parent_mean.shape), f32),
+            dma((LINKS, 2)),
+            dma((LINKS, RING)),
+            dma((LINKS, RING)),
+            dma((LINKS, RING)),
+            dma((2,)),
+            dma((LEVELS - 1,)),
+            dma((LEVELS - 1,)),
+            dma((4,)),
+            dma,
+            dma((children,)),
+            dma((LINKS * RING,)),
+            pltpu.SemaphoreType.REGULAR((LINKS,)),
+            pltpu.SemaphoreType.REGULAR((LINKS,)),
+        ],
+        compiler_params=pltpu.CompilerParams(
+            collective_id=0, has_side_effects=True, vmem_limit_bytes=63 << 20
+        ),
+    )(plan, items, config_weight, parent_tiles, parent_mean, factor_w, diag_inverse, own_mean)
+
+
+def any_reads(
     parent_tiles,
     parent_mean,
     factor_w,
@@ -70,6 +520,34 @@
     return (sigma_pj, sigma_jj, weight * variance, weight * mean_value)
 
 
+def shards(
+    parent_tiles,
+    parent_mean,
+    factor_w,
+    diag_inverse,
+    own_mean,
+    config_weight,
+    need_owner,
+    need_local,
+):
+    slots = need_owner[:, 0] * STORED + need_local
+    plan = pl.pallas_call(
+        plan_kernel,
+        out_shape=jax.ShapeDtypeStruct((8, SLOTS), jnp.int32),
+        in_specs=[pl.BlockSpec(memory_space=pltpu.VMEM)],
+        out_specs=pl.BlockSpec(memory_space=pltpu.VMEM),
+        scratch_shapes=[pltpu.VMEM((CHIPS, SLOTS), jnp.int32)] * 2,
+    )(slots.reshape(CHIPS, -1))
+    items = slots.shape[0] // lax.axis_size("front")
+    mine = lax.dynamic_slice_in_dim(slots, lax.axis_index("front") * items, items)
+    operands = (parent_tiles, parent_mean, factor_w, diag_inverse, own_mean, config_weight)
+    return lax.cond(
+        plan[2, 0] > 0,
+        lambda: exchange(plan, mine, *operands),
+        lambda: any_reads(*operands, need_owner, need_local),
+    )
+
+
 def solution(mesh):
     return jax.shard_map(
         shards,

time: 496 us -> 193 us (0.39)
  blocking collectives: 393 us -> 0 us
  Pallas kernels: 0 us -> 182 us
  local copies, waits for them, and re-layouts: 53.8 us -> 7.59 us
  matrix products: 20.5 us -> 0 us
  other arithmetic: 14.9 us -> 1.42 us
  starting transfers between devices: 11.3 us -> 0 us
    all_gather x1 -> x0, blocking collectives: 393 us -> none  [shards(): full_mean = lax.all_gather(parent_mean, 'front', axis=0, tiled=True)]
    pallas_call x0 -> x2, Pallas kernels: none -> 182 us  [the longest x1 176 us: exchange(): pl.pallas_call(exchange_kernel, out_shape=(jax.ShapeDtypeStruct(factor_w....]
    gather x7 -> x0, local copies, waits for them, and re-layouts: 27.7 us -> none  [the longest x1 13.6 us: shards(): jnp.take(received.reshape(fronts * capacity, tile_size, tile_size), arriv...]
    dot_general x3 -> x0, matrix products: 20.5 us -> none  [the longest x1 12.7 us: shards(): jnp.einsum('cabij,cbjk->caik', item_tiles, blocks, precision=highest_prec...]
    sub x1 -> x0, local copies, waits for them, and re-layouts: 17.2 us -> none  [shards(): diag_inverse - jnp.einsum('cpj,cpk->cjk', factor_w, sigma_pj, precision=h...]
    mul x3 -> x1, other arithmetic: 12.2 us -> 0.71 us  [shards(): slots = need_owner[:, 0] * STORED + need_local]
    all_to_all x1 -> x0, starting transfers between devices: 11.3 us -> none  [shards(): lax.all_to_all(tile_buffer, 'front', split_axis=0, concat_axis=0, tiled=T...]
  transfers between devices with their start and end apart: 1 -> 0, of which waited for: 0 -> 0; matrix products, arithmetic and copies ran while one was open for 1% -> 0% of each run, Pallas kernels for 0% -> 0%
where the time goes in v1:
time: 193 us
  Pallas kernels  182 us (94%)
  local copies, waits for them, and re-layouts  7.59 us (4%)
    pallas_call x1, Pallas kernels, exchange(): pl.pallas_call(exchange_kernel, out_shape=(jax.ShapeDtypeStruct(factor_w....  176 us
    pallas_call x1, Pallas kernels, shards(): pl.pallas_call(plan_kernel, out_shape=jax.ShapeDtypeStruct((8, SLOTS), jn...  6.1 us
    unnamed x4, local copies, waits for them, and re-layouts  5.82 us

profile of v1, /device:TPU:1, one launch (start us, length us, event | category | flops | bytes accessed | tf_op | source)
XLA Modules:
  0.0 192.8 jit_solution(13470656274068389166)
XLA Ops:
  0.6 0.7 multiply_reduce_fusion
  1.3 0.7 add.143
  2.1 0.7 reshape.239.slots_ref
  2.7 6.1 %shard_map.119 = s32[8,256]{1,0:T(8,128)S(1)} custom-call(s32[16,96]{1,0:T(8,128)} %reshape.239.slots_ref), custom_call_target="tpu_custom_call" | custom-call | tf_op jit(solution)/shard_map/pallas_call | solution.py:534
  8.8 0.5 slice.14
  10.0 177.0 %conditional.1 = (f32[3,1024,256]{2,1,0:T(8,128)}, f32[3,256]{1,0:T(4,128)S(1)}, f32[3,256,256]{2,1,0:T(8,128)S(1)}, f32[3,256]{1,0:T(4,128)S(1)}) conditional(s32[]{:T(128)} %bitcast.22, (s32[1536,1]{0,1:T(1,128)}, s32[1536]{0:T(1024)}, f32[8,256,256]{2,1,0:T(8,128)}, f32[3,1024,256]{2,1,0:T(8,128)}, f32[3,256,256]{2,1,0:T(8,128)}, ...), branch_computations={%region_0.4_spmd, %region_4.5_spmd} | conditional | flops 12101879808 | bytes 196637984 | solution.py:544
  10.2 0.6 dynamic_slice.13.item_ref
  10.8 176.1 %branch_1_fun.1 = (f32[3,1024,256]{2,1,0:T(8,128)}, f32[3,256,256]{2,1,0:T(8,128)S(1)}, f32[3,256]{1,0:T(4,128)S(1)}, f32[3,256]{1,0:T(4,128)S(1)}) custom-call(s32[8,256]{1,0:T(8,128)S(1)} %get-tuple-element.52.plan_ref, s32[48]{0:T(128)} %dynamic_slice.13.item_ref, f32[1]{0:T(128)} %get-tuple-element.55.weight_ref, ...), custom_call_target="tpu_custom_call" | custom-call | tf_op jit(solution)/shard_map/cond/branch_1_fun/pallas_call | solution.py:417
  187.0 3.8 %copy.69 = f32[3,1024,256]{2,1,0:T(8,128)} copy(f32[3,1024,256]{2,1,0:T(8,128)} %get-tuple-element.138) | data formatting | bytes 6291456
  190.7 0.9 copy.70
  191.6 0.6 copy.71
  192.2 0.6 copy.72

commit v2 on v1

--- a/solution.py
+++ b/solution.py
@@ -16,11 +16,13 @@
 CHIP_TILES = 16
 SLOTS = 256
 LINKS = 3
-WINDOWS = 26
+WINDOWS = 23
 POOL = CHIP_TILES + 2 * LINKS * WINDOWS
 RING = 4
 REACH = 5
 NONE = -1.0e6
+ROUNDS = 2
+STEEP = 0.03
 
 
 def split_bf16(value):
@@ -35,116 +37,132 @@
     return dot(left_high, right_high) + (dot(left_high, right_low) + dot(left_low, right_high))
 
 
-def plan_kernel(slots_ref, out_ref, table_ref, pool_ref):
+def swapped(value):
+    return jnp.concatenate([value[LEVELS:], value[:LEVELS]], axis=0)
+
+
+def turned(value, by):
+    return jnp.concatenate(
+        [pltpu.roll(value[:LEVELS], by, 0), pltpu.roll(value[LEVELS:], by, 0)], axis=0
+    )
+
+
+def most(value):
+    return jnp.max(value, axis=0, keepdims=True)
+
+
+def choose_routes(slots, uses_ref):
     shape = (CHIPS, SLOTS)
     row = lax.broadcasted_iota(jnp.int32, shape, 0)
     lane = lax.broadcasted_iota(jnp.int32, shape, 1)
+    one_lane = lax.broadcasted_iota(jnp.int32, (1, SLOTS), 1)
     chip_y, chip_z = row >> 3, row & 7
-    owner_y, owner_z, owner_core = lane >> 7, (lane >> 4) & 7, (lane >> 3) & 1
-    slots = slots_ref[...]
+    owner_y, owner_z = lane >> 7, (lane >> 4) & 7
     need = jnp.zeros(shape, jnp.float32)
     for item in range(slots.shape[1]):
         need = jnp.where(slots[:, item : item + 1] == lane, 1.0, need)
-
-    def swapped(value):
-        return jnp.concatenate([value[LEVELS:], value[:LEVELS]], axis=0)
-
-    def turned(value, by):
-        return jnp.concatenate(
-            [pltpu.roll(value[:LEVELS], by, 0), pltpu.roll(value[LEVELS:], by, 0)], axis=0
-        )
-
-    def most(value):
-        return jnp.max(value, axis=0, keepdims=True)
-
     other_need = swapped(need)
     level_need = jnp.maximum(need, other_need) > 0.0
     ahead = ((chip_z - owner_z) & 7).astype(jnp.float32)
     behind = ((owner_z - chip_z) & 7).astype(jnp.float32)
-    on_owner_line = chip_y == owner_y
-    one_lane = lax.broadcasted_iota(jnp.int32, (1, SLOTS), 1)
-    even = (one_lane & 1) == 0
-    best = jnp.full((1, SLOTS), 1.0e6, jnp.float32)
-    up = jnp.zeros((1, SLOTS), jnp.float32)
-    down = jnp.zeros((1, SLOTS), jnp.float32)
-    for cut in range(LEVELS - 1 - REACH, REACH + 1):
-        cut_up = most(jnp.where(level_need & (ahead <= cut), ahead, 0.0))
-        cut_down = most(jnp.where(level_need & (behind <= LEVELS - 1 - cut), behind, 0.0))
-        cost = (cut_up + cut_down) * 100.0 + jnp.abs(cut_up - cut_down) * 10.0
-        cost = cost + jnp.where((cut_up > cut_down) == even, 1.0, 0.0)
-        better = cost < best
-        best = jnp.where(better, cost, best)
-        up = jnp.where(better, cut_up, up)
-        down = jnp.where(better, cut_down, down)
-    own_count = jnp.sum(jnp.where(on_owner_line & (ahead > 0.0), need, 0.0), axis=0, keepdims=True)
-    other_count = jnp.sum(jnp.where(on_owner_line, 0.0, need), axis=0, keepdims=True)
-    crosses = jnp.where(other_count - own_count - 1.0 > 0.0, 1.0, 0.0)
-    on_line = jnp.where(on_owner_line, 1.0 - crosses, crosses) > 0.0
-    at_owner = on_owner_line & (ahead == 0.0)
-    at_level = ahead == 0.0
-    send_up = on_line & (ahead < up)
-    send_down = on_line & (behind < down)
-    reached = (ahead <= up) | (behind <= down)
-    crossing = at_owner & (crosses > 0.0)
-    send_over = crossing | (
-        on_line & reached & (other_need > 0.0) & jnp.logical_not(at_level & (crosses > 0.0))
-    )
-    end_up = most(jnp.where(on_line & (ahead == up), other_need, 0.0))
-    end_down = most(jnp.where(on_line & (behind == down), other_need, 0.0))
-    longest = jnp.maximum(2.0 * up + end_up, 2.0 * down + end_down)
-    rank_up = 2.0 * (up - ahead) + end_up
-    rank_down = 2.0 * (down - behind) + end_down
-    rank_over = jnp.where(crossing, longest + 2.0, 1.0)
-    key_up = jnp.where(send_up, rank_up * 256.0, NONE)
-    key_down = jnp.where(send_down, rank_down * 256.0, NONE)
-    key_over = jnp.where(send_over, rank_over * 256.0, NONE)
-    held = jnp.where(at_owner, (255 - (lane & 15)).astype(jnp.float32), NONE)
-
-    def window(w, carry):
-        keys, held, coming, table = list(carry[:3]), carry[3], carry[4], carry[5]
-        arrives = []
-        for link in range(LINKS):
-            sent = jnp.full(shape, NONE, jnp.float32)
-            for core in range(2):
-                key = keys[link] + held
-                key = jnp.where((owner_core == core) | (w >= 2), key, NONE)
-                top = jnp.max(key, axis=1, keepdims=True)
-                hit = (key == top) & (top > 0.0)
-                keys[link] = jnp.where(hit, NONE, keys[link])
-                place = CHIP_TILES + link * 2 * WINDOWS + 2 * w + core
-                sent = jnp.where(hit, (255 - place).astype(jnp.float32), sent)
-                found = jnp.where(top > 0.0, 255 - (top.astype(jnp.int32) & 255), 0)
-                table = jnp.where(lane == 6 * w + 2 * link + core, found, table)
-            arrives.append(sent)
-        fresh = jnp.maximum(
-            jnp.maximum(turned(arrives[0], 1), turned(arrives[1], LEVELS - 1)), swapped(arrives[2])
+    own_line = jnp.where(chip_y == owner_y, 1.0, 0.0)
+    at_level = jnp.where(ahead == 0.0, 1.0, 0.0)
+    at_owner = own_line * at_level
+    ups, downs = [], []
+    for option, cut in enumerate(range(LEVELS - 1 - REACH, REACH + 1)):
+        up = most(jnp.where(level_need & (ahead <= cut), ahead, 0.0))
+        down = most(jnp.where(level_need & (behind <= LEVELS - 1 - cut), behind, 0.0))
+        ups.append(up)
+        downs.append(down)
+        uses_ref[option, 0] = jnp.where(ahead < up, 1.0, 0.0)
+        uses_ref[option, 1] = jnp.where(behind < down, 1.0, 0.0)
+        reached = jnp.where((ahead <= up) | (behind <= down), other_need, 0.0)
+        uses_ref[option, 2] = reached * (1.0 - at_level * (1.0 - own_line))
+
+    def sends(up, down, crosses):
+        on_line = own_line * (1.0 - crosses) + (1.0 - own_line) * crosses
+        reached = jnp.where((ahead <= up) | (behind <= down), on_line * other_need, 0.0)
+        return (
+            jnp.where(ahead < up, on_line, 0.0),
+            jnp.where(behind < down, on_line, 0.0),
+            reached * (1.0 - at_level * crosses) + at_owner * crosses,
+            on_line,
         )
-        return (*keys, jnp.maximum(held, coming), fresh, table)
-
-    carry = (
-        key_up,
-        key_down,
-        key_over,
-        held,
+
+    def settle(step, carry):
+        choice, up, down, crosses = carry
+        steep = jnp.where(step == 0, 0.0, STEEP)
+        weights = [
+            jnp.exp(steep * (jnp.sum(use, axis=1, keepdims=True) - 40.0))
+            for use in sends(up, down, crosses)[:3]
+        ]
+        over = jnp.sum(at_owner * weights[2], axis=0, keepdims=True)
+        best = jnp.full((1, SLOTS), 1.0e9, jnp.float32)
+        chosen = [jnp.zeros((1, SLOTS), jnp.float32)] * 4
+        for option in range(len(ups)):
+            cost = sum(uses_ref[option, link] * weights[link] for link in range(LINKS))
+            first = jnp.sum(cost[:LEVELS], axis=0, keepdims=True)
+            second = jnp.sum(cost[LEVELS:], axis=0, keepdims=True)
+            for side in range(2):
+                total = jnp.where((one_lane < SLOTS // 2) == (side == 0), first, second)
+                total = total + over * float(side)
+                number = 2.0 * option + side
+                total = jnp.where(choice == number, total - 0.1, total)
+                better = total < best
+                best = jnp.where(better, total, best)
+                values = (number, ups[option], downs[option], float(side))
+                chosen = [jnp.where(better, v, c) for v, c in zip(values, chosen)]
+        turn = ((one_lane & 15) == ((step - 1) & 15)) | (step == 0)
+        return tuple(jnp.where(turn, c, old) for c, old in zip(chosen, carry))
+
+    start = (jnp.full((1, SLOTS), -1.0, jnp.float32),) + (jnp.zeros((1, SLOTS), jnp.float32),) * 3
+    choice, up, down, crosses = lax.fori_loop(0, 1 + 16 * ROUNDS, settle, start)
+    send_up, send_down, send_over, on_line = sends(up, down, crosses)
+    end_up = most(jnp.where(ahead == up, on_line * other_need, 0.0))
+    end_down = most(jnp.where(behind == down, on_line * other_need, 0.0))
+    longest = jnp.maximum(2.0 * up + 3.0 * end_up, 2.0 * down + 3.0 * end_down)
+    rank_up = 2.0 * (up - ahead) + 3.0 * end_up + 2.0 * turned(other_need, LEVELS - 1)
+    rank_down = 2.0 * (down - behind) + 3.0 * end_down + 2.0 * turned(other_need, 1)
+    rank_over = jnp.where(at_owner * crosses > 0.0, longest + 2.0, 1.0)
+    return (
+        jnp.where(send_up > 0.0, rank_up * 256.0, NONE),
+        jnp.where(send_down > 0.0, rank_down * 256.0, NONE),
+        jnp.where(send_over > 0.0, rank_over * 256.0, NONE),
+        jnp.where(at_owner > 0.0, (255 - (lane & 15)).astype(jnp.float32), NONE),
         jnp.full(shape, NONE, jnp.float32),
         jnp.zeros(shape, jnp.int32),
     )
-    key_up, key_down, key_over, held, coming, table = lax.fori_loop(0, WINDOWS, window, carry)
-    held = jnp.maximum(held, coming)
-    table_ref[...] = table
-    pool_ref[...] = jnp.where(held >= 0.0, 255 - held.astype(jnp.int32), 0)
-    left = jnp.maximum(jnp.maximum(key_up, key_down), key_over)
-    fits = jnp.where(jnp.max(left) > 0.0, 0, 1)
-    chip = lax.axis_index("front") // 2
-    out_ref[...] = jnp.zeros(out_ref.shape, jnp.int32)
-    out_ref[0:1, :] = table_ref[pl.ds(chip, 1), :]
-    out_ref[1:2, :] = pool_ref[pl.ds(chip, 1), :]
-    out_ref[2:3, :] = jnp.full((1, SLOTS), fits, jnp.int32)
+
+
+def schedule(w, carry):
+    keys, held, coming, table = list(carry[:3]), carry[3], carry[4], carry[5]
+    shape = held.shape
+    lane = lax.broadcasted_iota(jnp.int32, shape, 1)
+    arrives = []
+    for link in range(LINKS):
+        sent = jnp.full(shape, NONE, jnp.float32)
+        for core in range(2):
+            key = keys[link] + held
+            key = jnp.where((((lane >> 3) & 1) == core) | (w >= 2), key, NONE)
+            top = jnp.max(key, axis=1, keepdims=True)
+            hit = (key == top) & (top > 0.0)
+            keys[link] = jnp.where(hit, NONE, keys[link])
+            place = CHIP_TILES + link * 2 * WINDOWS + 2 * w + core
+            sent = jnp.where(hit, jnp.asarray(255 - place).astype(jnp.float32), sent)
+            found = jnp.where(top > 0.0, 255 - (top.astype(jnp.int32) & 255), 0)
+            table = jnp.where(lane == 6 * w + 2 * link + core, found, table)
+        arrives.append(sent)
+    fresh = jnp.maximum(
+        jnp.maximum(turned(arrives[0], 1), turned(arrives[1], LEVELS - 1)), swapped(arrives[2])
+    )
+    return (*keys, jnp.maximum(held, coming), fresh, table)
 
 
 def exchange_kernel(
-    plan_ref,
-    item_ref,
+    owner_ref,
+    local_ref,
+    owner_item_ref,
+    local_item_ref,
     weight_ref,
     tiles_ref,
     mean_ref,
@@ -155,6 +173,7 @@
     jj_ref,
     variance_ref,
     out_mean_ref,
+    fits_ref,
     pool,
     land,
     passed,
@@ -166,6 +185,11 @@
     stage,
     jj,
     means,
+    uses,
+    whole,
+    rows_out,
+    first_plan,
+    plan,
     send_sem,
     land_sem,
     pass_send_sem,
@@ -177,6 +201,7 @@
     stage_sem,
     jj_sem,
     out_sem,
+    plan_sem,
     credit,
     pass_credit,
 ):
@@ -218,6 +243,17 @@
         signal(barrier, neighbour)
     line = y * 2 + core
     means[line, z] = mean_ref[...]
+    routes = choose_routes(owner_ref[...] * STORED + local_ref[...], uses)
+    routes = lax.fori_loop(0, 2, schedule, routes)
+
+    def own_row(at, values):
+        whole[...] = values
+        rows_out[at : at + 1, :] = whole[pl.ds(me // 2, 1), :]
+
+    own_row(0, routes[5])
+    first_copy = pltpu.make_async_copy(rows_out, first_plan, plan_sem)
+    first_copy.start()
+    first_copy.wait()
     pl.semaphore_wait(barrier, 4)
 
     own = pl.ds(core * STORED, STORED)
@@ -246,9 +282,12 @@
             partner,
         )
 
+    def planned(table, w, link):
+        return jnp.clip(table[0, 6 * w + 2 * link + core], 0, POOL - 1)
+
     for w in range(2):
         for link in range(LINKS):
-            outgoing[link, w] = tiles_ref[plan_ref[0, 6 * w + 2 * link + core] % STORED]
+            outgoing[link, w] = tiles_ref[planned(first_plan, w, link) % STORED]
             send(w, link).start()
         if w == 0:
             swap.start()
@@ -259,6 +298,15 @@
         return carry
 
     lax.fori_loop(0, STORED, keep, 0)
+    key_up, key_down, key_over, held, coming, table = lax.fori_loop(2, WINDOWS, schedule, routes)
+    held = jnp.maximum(held, coming)
+    own_row(0, table)
+    own_row(1, jnp.where(held >= 0.0, 255 - held.astype(jnp.int32), 0))
+    plan_copy = pltpu.make_async_copy(rows_out, plan, plan_sem)
+    plan_copy.start()
+    left = jnp.maximum(jnp.maximum(key_up, key_down), key_over)
+    fits_ref[0] = jnp.where(jnp.max(left) > 0.0, 0, 1)
+    plan_copy.wait()
     swap.wait()
 
     def take(v):
@@ -293,11 +341,29 @@
     line_swap = remote(means.at[line], means.at[line], mean_sem.at[0], mean_sem.at[1], partner)
     mean_swap = remote(both, both, mean_sem.at[2], mean_sem.at[3], across)
 
+    def slot_of(item):
+        at = core * (children * 16) + item
+        return owner_item_ref[me // 2, at] * STORED + local_item_ref[me // 2, at]
+
+    weight = weight_ref[0]
+
+    def weigh_mean(child):
+        total = jnp.zeros((16, 256), jnp.float32)
+        for a in range(4):
+            slot = slot_of(child * 16 + a * 5)
+            slot_line = slot // 128 * 2 + slot // 8 % 2
+            piece = means[slot_line, slot // 16 % 8, pl.ds(slot % 8, 1), :]
+            piece_high, piece_low = split_bf16(jnp.broadcast_to(piece, (16, 256)))
+            rows = pl.ds(child * 1024 + a * 256, 256)
+            total += dot3(piece_high, piece_low, high[rows, :], low[rows, :])
+        value = own_mean_ref[pl.ds(child, 1), :] - total[0:1]
+        out_mean_ref[pl.ds(child, 1), :] = weight * value
+
     def window(w, carry):
         take(w - 2)
         for link in range(LINKS):
             send(w, link).wait_send()
-            outgoing[link, w % 2] = pool[plan_ref[0, 6 * w + 2 * link + core]]
+            outgoing[link, w % 2] = pool[planned(plan, w, link)]
 
             @pl.when(w >= RING)
             def _():
@@ -325,6 +391,10 @@
         @pl.when(w == 11)
         def _():
             mean_swap.wait()
+
+        @pl.when((w >= 12) & (w < 12 + children))
+        def _():
+            weigh_mean(w - 12)
 
         @pl.when((w >= 3) & (w < 3 + children))
         def _():
@@ -352,7 +422,6 @@
             send(w, link).wait_send()
     jj_load.wait()
 
-    weight = weight_ref[0]
     rows_at = lax.broadcasted_iota(jnp.int32, (256, 256), 0)
     cols_at = lax.broadcasted_iota(jnp.int32, (256, 256), 1)
 
@@ -368,7 +437,7 @@
         def pattern_row(a, carry):
             total = jnp.zeros((256, 256), jnp.float32)
             for b in range(4):
-                item = plan_ref[1, item_ref[child * 16 + a * 4 + b]]
+                item = jnp.clip(plan[1, slot_of(child * 16 + a * 4 + b)], 0, POOL - 1)
                 tile_high, tile_low = split_bf16(pool[item])
                 rows = pl.ds(child * 1024 + b * 256, 256)
                 total += dot3(tile_high, tile_low, high[rows, :], low[rows, :])
@@ -387,16 +456,6 @@
         jj_out(child).start()
         diagonal = jnp.where(rows_at == cols_at, jj[child], 0.0)
         variance_ref[pl.ds(child, 1), :] = weight * jnp.sum(diagonal, axis=0, keepdims=True)
-        total = jnp.zeros((16, 256), jnp.float32)
-        for a in range(4):
-            slot = item_ref[child * 16 + a * 5]
-            slot_line = slot // 128 * 2 + slot // 8 % 2
-            piece = means[slot_line, slot // 16 % 8, pl.ds(slot % 8, 1), :]
-            piece_high, piece_low = split_bf16(jnp.broadcast_to(piece, (16, 256)))
-            rows = pl.ds(child * 1024 + a * 256, 256)
-            total += dot3(piece_high, piece_low, high[rows, :], low[rows, :])
-        value = own_mean_ref[pl.ds(child, 1), :] - total[0:1]
-        out_mean_ref[pl.ds(child, 1), :] = weight * value
         return carry
 
     lax.fori_loop(0, children, front, 0)
@@ -406,7 +465,7 @@
         jj_out(child).wait()
 
 
-def exchange(plan, items, parent_tiles, parent_mean, factor_w, diag_inverse, own_mean, config_weight):
+def exchange(owners, locals_, parent_tiles, parent_mean, factor_w, diag_inverse, own_mean, config_weight):
     tile = parent_tiles.shape[1:]
     children, depth, width = factor_w.shape
     vmem = pl.BlockSpec(memory_space=pltpu.VMEM)
@@ -421,9 +480,10 @@
             jax.ShapeDtypeStruct(diag_inverse.shape, f32),
             jax.ShapeDtypeStruct(own_mean.shape, f32),
             jax.ShapeDtypeStruct(own_mean.shape, f32),
+            jax.ShapeDtypeStruct((1,), jnp.int32),
         ),
-        in_specs=[smem, smem, smem, vmem, vmem, anywhere, anywhere, vmem],
-        out_specs=(anywhere, anywhere, vmem, vmem),
+        in_specs=[vmem, vmem, smem, smem, smem, vmem, vmem, anywhere, anywhere, vmem],
+        out_specs=(anywhere, anywhere, vmem, vmem, smem),
         scratch_shapes=[
             pltpu.VMEM((POOL, *tile), f32),
             pltpu.VMEM((LINKS * RING, *tile), f32),
@@ -436,6 +496,11 @@
             pltpu.VMEM((depth, width), f32),
             pltpu.VMEM(diag_inverse.shape, f32),
             pltpu.VMEM((4, LEVELS, *parent_mean.shape), f32),
+            pltpu.VMEM((2 * REACH - LEVELS + 2, LINKS, CHIPS, SLOTS), f32),
+            pltpu.VMEM((CHIPS, SLOTS), jnp.int32),
+            pltpu.VMEM((8, SLOTS), jnp.int32),
+            pltpu.SMEM((8, SLOTS), jnp.int32),
+            pltpu.SMEM((8, SLOTS), jnp.int32),
             dma((LINKS, 2)),
             dma((LINKS, RING)),
             dma((LINKS, RING)),
@@ -447,13 +512,25 @@
             dma,
             dma((children,)),
             dma((LINKS * RING,)),
+            dma,
             pltpu.SemaphoreType.REGULAR((LINKS,)),
             pltpu.SemaphoreType.REGULAR((LINKS,)),
         ],
         compiler_params=pltpu.CompilerParams(
             collective_id=0, has_side_effects=True, vmem_limit_bytes=63 << 20
         ),
-    )(plan, items, config_weight, parent_tiles, parent_mean, factor_w, diag_inverse, own_mean)
+    )(
+        owners,
+        locals_,
+        owners,
+        locals_,
+        config_weight,
+        parent_tiles,
+        parent_mean,
+        factor_w,
+        diag_inverse,
+        own_mean,
+    )
 
 
 def any_reads(
@@ -520,6 +597,30 @@
     return (sigma_pj, sigma_jj, weight * variance, weight * mean_value)
 
 
+def finish_kernel(*refs):
+    count = len(refs) // 2
+    for source, result in zip(refs[:count], refs[count:]):
+        result[...] = source[...]
+
+
+def finish(*values):
+    children, depth, width = values[0].shape
+    parts = 2
+    specs = (
+        pl.BlockSpec((1, depth // parts, width), lambda step: (step // parts, step % parts, 0)),
+        pl.BlockSpec((1, width // parts, width), lambda step: (step // parts, step % parts, 0)),
+        pl.BlockSpec((children, width), lambda step: (0, 0)),
+        pl.BlockSpec((children, width), lambda step: (0, 0)),
+    )
+    return pl.pallas_call(
+        finish_kernel,
+        grid=(children * parts,),
+        out_shape=tuple(jax.ShapeDtypeStruct(value.shape, value.dtype) for value in values),
+        in_specs=specs,
+        out_specs=specs,
+    )(*values)
+
+
 def shards(
     parent_tiles,
     parent_mean,
@@ -530,20 +631,13 @@
     need_owner,
     need_local,
 ):
-    slots = need_owner[:, 0] * STORED + need_local
-    plan = pl.pallas_call(
-        plan_kernel,
-        out_shape=jax.ShapeDtypeStruct((8, SLOTS), jnp.int32),
-        in_specs=[pl.BlockSpec(memory_space=pltpu.VMEM)],
-        out_specs=pl.BlockSpec(memory_space=pltpu.VMEM),
-        scratch_shapes=[pltpu.VMEM((CHIPS, SLOTS), jnp.int32)] * 2,
-    )(slots.reshape(CHIPS, -1))
-    items = slots.shape[0] // lax.axis_size("front")
-    mine = lax.dynamic_slice_in_dim(slots, lax.axis_index("front") * items, items)
     operands = (parent_tiles, parent_mean, factor_w, diag_inverse, own_mean, config_weight)
+    *outputs, fits = exchange(
+        need_owner.reshape(CHIPS, -1), need_local.reshape(CHIPS, -1), *operands
+    )
     return lax.cond(
-        plan[2, 0] > 0,
-        lambda: exchange(plan, mine, *operands),
+        fits[0] > 0,
+        lambda: tuple(finish(*outputs)),
         lambda: any_reads(*operands, need_owner, need_local),
     )
 

time: 193 us -> 175 us (0.907)
  Pallas kernels: 182 us -> 170 us
  local copies, waits for them, and re-layouts: 7.59 us -> 2.04 us
    pallas_call x1, Pallas kernels: 176 us -> 164 us  [exchange(): pl.pallas_call(exchange_kernel, out_shape=(jax.ShapeDtypeStruct(factor_w....]
    unnamed x4 -> x0, local copies, waits for them, and re-layouts: 5.82 us -> none
where the time goes in v2:
time: 175 us
  Pallas kernels  170 us (97%)
  between operations  2.15 us (1%)
  local copies, waits for them, and re-layouts  2.04 us (1%)
    pallas_call x1, Pallas kernels, exchange(): pl.pallas_call(exchange_kernel, out_shape=(jax.ShapeDtypeStruct(factor_w....  164 us
    pallas_call x1, Pallas kernels, finish(): pl.pallas_call(finish_kernel, grid=(children * parts,), out_shape=tuple((...  5.57 us

profile of v2, /device:TPU:1, one launch (start us, length us, event | category | flops | bytes accessed | tf_op | source)
XLA Modules:
  0.0 174.8 jit_solution(840542311357162888)
XLA Ops:
  0.6 0.7 reduce.2
  1.3 0.7 reshape.240.owner_ref.owner_item_ref
  2.0 1.4 reshape.241.local_ref.local_item_ref
  4.0 164.1 %shard_map.119 = (f32[3,1024,256]{2,1,0:T(8,128)}, f32[3,256,256]{2,1,0:T(8,128)}, f32[3,256]{1,0:T(4,128)S(1)}, f32[3,256]{1,0:T(4,128)S(1)}, s32[1]{0:T(128)}) custom-call(s32[16,96]{1,0:T(8,128)} %reshape.240.owner_ref.owner_item_ref, s32[16,96]{1,0:T(8,128)} %reshape.241.local_ref.local_item_ref, s32[16,96]{1,0:T(8,128)} %reshape.240.owner_ref.owner_item_ref, ...), custom_call_target="tpu_custom_call" | custom-call | tf_op jit(solution)/shard_map/pallas_call | solution.py:476
  168.8 5.8 %conditional.1 = (f32[3,1024,256]{2,1,0:T(8,128)}, f32[3,256]{1,0:T(4,128)}, f32[3,256,256]{2,1,0:T(8,128)}, f32[3,256]{1,0:T(4,128)}) conditional(s32[]{:T(128)} %bitcast.22, (s32[1536,1]{0,1:T(1,128)}, s32[1536]{0:T(1024)}, f32[8,256,256]{2,1,0:T(8,128)}, f32[3,1024,256]{2,1,0:T(8,128)}, f32[3,256,256]{2,1,0:T(8,128)}, /*index=5*/f32[1]{0:T(128)}, ...), branch_computations={%region_0.4_spmd, %region_4.5_spmd} | conditional | flops 12101879808 | bytes 209220928 | solution.py:638
  169.0 5.6 %branch_1_fun.1 = (f32[3,1024,256]{2,1,0:T(8,128)}, f32[3,256,256]{2,1,0:T(8,128)}, f32[3,256]{1,0:T(4,128)}, f32[3,256]{1,0:T(4,128)}) custom-call(f32[3,1024,256]{2,1,0:T(8,128)} %get-tuple-element.32.refs_0_, f32[3,256,256]{2,1,0:T(8,128)} %get-tuple-element.33.refs_1_, f32[3,256]{1,0:T(4,128)S(1)} %get-tuple-element.34.refs_2_, ...), custom_call_target="tpu_custom_call" | custom-call | tf_op jit(solution)/shard_map/cond/branch_1_fun/pallas_call | solution.py:615

commit v3 on v2

--- a/solution.py
+++ b/solution.py
@@ -22,6 +22,7 @@
 REACH = 5
 NONE = -1.0e6
 ROUNDS = 2
+EARLY = 10
 STEEP = 0.03
 
 
@@ -51,7 +52,7 @@
     return jnp.max(value, axis=0, keepdims=True)
 
 
-def choose_routes(slots, uses_ref):
+def planner(slots, uses_ref):
     shape = (CHIPS, SLOTS)
     row = lax.broadcasted_iota(jnp.int32, shape, 0)
     lane = lax.broadcasted_iota(jnp.int32, shape, 1)
@@ -68,6 +69,7 @@
     own_line = jnp.where(chip_y == owner_y, 1.0, 0.0)
     at_level = jnp.where(ahead == 0.0, 1.0, 0.0)
     at_owner = own_line * at_level
+    needed_over = most(at_owner * other_need)
     ups, downs = [], []
     for option, cut in enumerate(range(LEVELS - 1 - REACH, REACH + 1)):
         up = most(jnp.where(level_need & (ahead <= cut), ahead, 0.0))
@@ -89,7 +91,7 @@
             on_line,
         )
 
-    def settle(step, carry):
+    def settle(step, carry, kept=None):
         choice, up, down, crosses = carry
         steep = jnp.where(step == 0, 0.0, STEEP)
         weights = [
@@ -108,6 +110,15 @@
                 total = total + over * float(side)
                 number = 2.0 * option + side
                 total = jnp.where(choice == number, total - 0.1, total)
+                if kept is not None:
+                    kept_up, kept_down, kept_over = kept
+                    if side == 0:
+                        broken = kept_over * (1.0 - needed_over)
+                        broken = broken + jnp.where(ups[option] == 0.0, kept_up, 0.0)
+                        broken = broken + jnp.where(downs[option] == 0.0, kept_down, 0.0)
+                    else:
+                        broken = kept_up + kept_down
+                    total = total + 1.0e4 * broken
                 better = total < best
                 best = jnp.where(better, total, best)
                 values = (number, ups[option], downs[option], float(side))
@@ -115,23 +126,29 @@
         turn = ((one_lane & 15) == ((step - 1) & 15)) | (step == 0)
         return tuple(jnp.where(turn, c, old) for c, old in zip(chosen, carry))
 
-    start = (jnp.full((1, SLOTS), -1.0, jnp.float32),) + (jnp.zeros((1, SLOTS), jnp.float32),) * 3
-    choice, up, down, crosses = lax.fori_loop(0, 1 + 16 * ROUNDS, settle, start)
-    send_up, send_down, send_over, on_line = sends(up, down, crosses)
-    end_up = most(jnp.where(ahead == up, on_line * other_need, 0.0))
-    end_down = most(jnp.where(behind == down, on_line * other_need, 0.0))
-    longest = jnp.maximum(2.0 * up + 3.0 * end_up, 2.0 * down + 3.0 * end_down)
-    rank_up = 2.0 * (up - ahead) + 3.0 * end_up + 2.0 * turned(other_need, LEVELS - 1)
-    rank_down = 2.0 * (down - behind) + 3.0 * end_down + 2.0 * turned(other_need, 1)
-    rank_over = jnp.where(at_owner * crosses > 0.0, longest + 2.0, 1.0)
-    return (
-        jnp.where(send_up > 0.0, rank_up * 256.0, NONE),
-        jnp.where(send_down > 0.0, rank_down * 256.0, NONE),
-        jnp.where(send_over > 0.0, rank_over * 256.0, NONE),
+    def ranked(carry):
+        choice, up, down, crosses = carry
+        send_up, send_down, send_over, on_line = sends(up, down, crosses)
+        end_up = most(jnp.where(ahead == up, on_line * other_need, 0.0))
+        end_down = most(jnp.where(behind == down, on_line * other_need, 0.0))
+        longest = jnp.maximum(2.0 * up + 3.0 * end_up, 2.0 * down + 3.0 * end_down)
+        rank_up = 2.0 * (up - ahead) + 3.0 * end_up + 2.0 * turned(other_need, LEVELS - 1)
+        rank_down = 2.0 * (down - behind) + 3.0 * end_down + 2.0 * turned(other_need, 1)
+        rank_over = jnp.where(at_owner * crosses > 0.0, longest + 2.0, 1.0)
+        return (
+            jnp.where(send_up > 0.0, rank_up * 256.0, NONE),
+            jnp.where(send_down > 0.0, rank_down * 256.0, NONE),
+            jnp.where(send_over > 0.0, rank_over * 256.0, NONE),
+        )
+
+    unchosen = (jnp.full((1, SLOTS), -1.0, jnp.float32),)
+    unchosen = unchosen + (jnp.zeros((1, SLOTS), jnp.float32),) * 3
+    at_start = (
         jnp.where(at_owner > 0.0, (255 - (lane & 15)).astype(jnp.float32), NONE),
         jnp.full(shape, NONE, jnp.float32),
         jnp.zeros(shape, jnp.int32),
     )
+    return settle, ranked, unchosen, at_start
 
 
 def schedule(w, carry):
@@ -143,7 +160,7 @@
         sent = jnp.full(shape, NONE, jnp.float32)
         for core in range(2):
             key = keys[link] + held
-            key = jnp.where((((lane >> 3) & 1) == core) | (w >= 2), key, NONE)
+            key = jnp.where((((lane >> 3) & 1) == core) | (jnp.asarray(w) >= 2), key, NONE)
             top = jnp.max(key, axis=1, keepdims=True)
             hit = (key == top) & (top > 0.0)
             keys[link] = jnp.where(hit, NONE, keys[link])
@@ -183,7 +200,7 @@
     turned_high,
     turned_low,
     stage,
-    jj,
+    mine,
     means,
     uses,
     whole,
@@ -200,8 +217,8 @@
     mean_sem,
     stage_sem,
     jj_sem,
-    out_sem,
     plan_sem,
+    tiles_sem,
     credit,
     pass_credit,
 ):
@@ -235,7 +252,9 @@
     def load_stage(child):
         return pltpu.make_async_copy(factor_ref.at[child], stage, stage_sem)
 
-    jj_load = pltpu.make_async_copy(diag_ref, jj, jj_sem.at[0])
+    jj_load = pltpu.make_async_copy(diag_ref, jj_ref, jj_sem.at[0])
+    tiles_load = pltpu.make_async_copy(tiles_ref, mine, tiles_sem)
+    tiles_load.start()
     load_stage(0).start()
     jj_load.start()
     barrier = pltpu.get_barrier_semaphore()
@@ -243,21 +262,31 @@
         signal(barrier, neighbour)
     line = y * 2 + core
     means[line, z] = mean_ref[...]
-    routes = choose_routes(owner_ref[...] * STORED + local_ref[...], uses)
-    routes = lax.fori_loop(0, 2, schedule, routes)
+    settle, ranked, unchosen, at_start = planner(owner_ref[...] * STORED + local_ref[...], uses)
+    chosen = settle(0, unchosen)
+    first_keys = ranked(chosen)
+    after = schedule(0, (*first_keys, *at_start))
+    gone = [(old > 0.0) & (new < 0.0) for old, new in zip(first_keys, after)]
+    kept = [most(jnp.where(sent, 1.0, 0.0)) for sent in gone]
 
     def own_row(at, values):
         whole[...] = values
         rows_out[at : at + 1, :] = whole[pl.ds(me // 2, 1), :]
 
-    own_row(0, routes[5])
+    own_row(0, after[5])
     first_copy = pltpu.make_async_copy(rows_out, first_plan, plan_sem)
     first_copy.start()
+
+    def resettle(step, carry):
+        return settle(step, carry, kept)
+
+    chosen = lax.fori_loop(1, 1 + EARLY, resettle, chosen)
     first_copy.wait()
+    tiles_load.wait()
     pl.semaphore_wait(barrier, 4)
 
     own = pl.ds(core * STORED, STORED)
-    swap = remote(tiles_ref, pool.at[own], swap_sem.at[0], swap_sem.at[1], partner)
+    swap = remote(mine, pool.at[own], swap_sem.at[0], swap_sem.at[1], partner)
 
     def ring(step):
         block = means.at[line, (z + 8 - step) % 8]
@@ -285,16 +314,25 @@
     def planned(table, w, link):
         return jnp.clip(table[0, 6 * w + 2 * link + core], 0, POOL - 1)
 
-    for w in range(2):
+    def send_own(w, table):
         for link in range(LINKS):
-            outgoing[link, w] = tiles_ref[planned(first_plan, w, link) % STORED]
+            outgoing[link, w] = mine[planned(table, w, link) % STORED]
             send(w, link).start()
-        if w == 0:
-            swap.start()
-            ring(0).start()
+
+    send_own(0, first_plan)
+    swap.start()
+    ring(0).start()
+    chosen = lax.fori_loop(1 + EARLY, 1 + 16 * ROUNDS, resettle, chosen)
+    keys = [jnp.where(sent, NONE, key) for sent, key in zip(gone, ranked(chosen))]
+    routes = schedule(1, (*keys, *after[3:]))
+    own_row(0, routes[5])
+    plan_copy = pltpu.make_async_copy(rows_out, plan, plan_sem)
+    plan_copy.start()
+    plan_copy.wait()
+    send_own(1, plan)
 
     def keep(tile, carry):
-        pool[core * STORED + tile] = tiles_ref[tile]
+        pool[core * STORED + tile] = mine[tile]
         return carry
 
     lax.fori_loop(0, STORED, keep, 0)
@@ -302,7 +340,6 @@
     held = jnp.maximum(held, coming)
     own_row(0, table)
     own_row(1, jnp.where(held >= 0.0, 255 - held.astype(jnp.int32), 0))
-    plan_copy = pltpu.make_async_copy(rows_out, plan, plan_sem)
     plan_copy.start()
     left = jnp.maximum(jnp.maximum(key_up, key_down), key_over)
     fits_ref[0] = jnp.where(jnp.max(left) > 0.0, 0, 1)
@@ -425,14 +462,6 @@
     rows_at = lax.broadcasted_iota(jnp.int32, (256, 256), 0)
     cols_at = lax.broadcasted_iota(jnp.int32, (256, 256), 1)
 
-    def pj_out(place):
-        return pltpu.make_async_copy(
-            land.at[place], pj_ref.at[place // 4, pl.ds((place % 4) * 256, 256)], out_sem.at[place]
-        )
-
-    def jj_out(child):
-        return pltpu.make_async_copy(jj.at[child], jj_ref.at[child], jj_sem.at[child])
-
     def front(child, carry):
         def pattern_row(a, carry):
             total = jnp.zeros((256, 256), jnp.float32)
@@ -442,27 +471,20 @@
                 rows = pl.ds(child * 1024 + b * 256, 256)
                 total += dot3(tile_high, tile_low, high[rows, :], low[rows, :])
             block = -total
-            place = child * 4 + a
-            land[place] = block
-            pj_out(place).start()
+            pj_ref[child, pl.ds(pl.multiple_of(a * 256, 256), 256), :] = block
             block_high, block_low = split_bf16(block)
             cols = pl.ds(pl.multiple_of(a * 256, 256), 256)
-            jj[child] -= dot3(
+            jj_ref[child] -= dot3(
                 turned_high[child, :, cols], turned_low[child, :, cols], block_high, block_low
             )
             return carry
 
         lax.fori_loop(0, 4, pattern_row, 0)
-        jj_out(child).start()
-        diagonal = jnp.where(rows_at == cols_at, jj[child], 0.0)
+        diagonal = jnp.where(rows_at == cols_at, jj_ref[child], 0.0)
         variance_ref[pl.ds(child, 1), :] = weight * jnp.sum(diagonal, axis=0, keepdims=True)
         return carry
 
     lax.fori_loop(0, children, front, 0)
-    for child in range(children):
-        for a in range(4):
-            pj_out(child * 4 + a).wait()
-        jj_out(child).wait()
 
 
 def exchange(owners, locals_, parent_tiles, parent_mean, factor_w, diag_inverse, own_mean, config_weight):
@@ -476,14 +498,14 @@
     return pl.pallas_call(
         exchange_kernel,
         out_shape=(
-            jax.ShapeDtypeStruct(factor_w.shape, f32),
+            pltpu.VMEM(factor_w.shape, f32),
             jax.ShapeDtypeStruct(diag_inverse.shape, f32),
             jax.ShapeDtypeStruct(own_mean.shape, f32),
             jax.ShapeDtypeStruct(own_mean.shape, f32),
             jax.ShapeDtypeStruct((1,), jnp.int32),
         ),
-        in_specs=[vmem, vmem, smem, smem, smem, vmem, vmem, anywhere, anywhere, vmem],
-        out_specs=(anywhere, anywhere, vmem, vmem, smem),
+        in_specs=[vmem, vmem, smem, smem, smem, anywhere, vmem, anywhere, anywhere, vmem],
+        out_specs=(vmem, vmem, vmem, vmem, smem),
         scratch_shapes=[
             pltpu.VMEM((POOL, *tile), f32),
             pltpu.VMEM((LINKS * RING, *tile), f32),
@@ -494,7 +516,7 @@
             pltpu.VMEM((children, width, depth), bf16),
             pltpu.VMEM((children, width, depth), bf16),
             pltpu.VMEM((depth, width), f32),
-            pltpu.VMEM(diag_inverse.shape, f32),
+            pltpu.VMEM((STORED, *tile), f32),
             pltpu.VMEM((4, LEVELS, *parent_mean.shape), f32),
             pltpu.VMEM((2 * REACH - LEVELS + 2, LINKS, CHIPS, SLOTS), f32),
             pltpu.VMEM((CHIPS, SLOTS), jnp.int32),
@@ -511,13 +533,13 @@
             dma((4,)),
             dma,
             dma((children,)),
-            dma((LINKS * RING,)),
+            dma,
             dma,
             pltpu.SemaphoreType.REGULAR((LINKS,)),
             pltpu.SemaphoreType.REGULAR((LINKS,)),
         ],
         compiler_params=pltpu.CompilerParams(
-            collective_id=0, has_side_effects=True, vmem_limit_bytes=63 << 20
+            collective_id=0, has_side_effects=True, vmem_limit_bytes=58 << 20
         ),
     )(
         owners,
@@ -597,28 +619,30 @@
     return (sigma_pj, sigma_jj, weight * variance, weight * mean_value)
 
 
-def finish_kernel(*refs):
-    count = len(refs) // 2
-    for source, result in zip(refs[:count], refs[count:]):
-        result[...] = source[...]
+def finish_kernel(pj_ref, jj_ref, variance_ref, mean_ref, *refs):
+    pj_out, jj_out, variance_out, mean_out, sems = refs
+    copies = [
+        pltpu.make_async_copy(pj_ref, pj_out, sems.at[0]),
+        pltpu.make_async_copy(jj_ref, jj_out, sems.at[1]),
+    ]
+    for copy in copies:
+        copy.start()
+    variance_out[...] = variance_ref[...]
+    mean_out[...] = mean_ref[...]
+    for copy in copies:
+        copy.wait()
 
 
 def finish(*values):
-    children, depth, width = values[0].shape
-    parts = 2
-    specs = (
-        pl.BlockSpec((1, depth // parts, width), lambda step: (step // parts, step % parts, 0)),
-        pl.BlockSpec((1, width // parts, width), lambda step: (step // parts, step % parts, 0)),
-        pl.BlockSpec((children, width), lambda step: (0, 0)),
-        pl.BlockSpec((children, width), lambda step: (0, 0)),
-    )
+    vmem = pl.BlockSpec(memory_space=pltpu.VMEM)
+    anywhere = pl.BlockSpec(memory_space=pl.ANY)
     return pl.pallas_call(
         finish_kernel,
-        grid=(children * parts,),
         out_shape=tuple(jax.ShapeDtypeStruct(value.shape, value.dtype) for value in values),
-        in_specs=specs,
-        out_specs=specs,
-    )(*values)
+        in_specs=[vmem] * 4,
+        out_specs=(anywhere, anywhere, vmem, vmem),
+        scratch_shapes=[pltpu.SemaphoreType.DMA((2,))],
+    )(pltpu.with_memory_space_constraint(values[0], pltpu.VMEM), *values[1:])
 
 
 def shards(
@@ -635,9 +659,10 @@
     *outputs, fits = exchange(
         need_owner.reshape(CHIPS, -1), need_local.reshape(CHIPS, -1), *operands
     )
+    done = tuple(finish(*outputs))
     return lax.cond(
         fits[0] > 0,
-        lambda: tuple(finish(*outputs)),
+        lambda: done,
         lambda: any_reads(*operands, need_owner, need_local),
     )
 

time: 175 us -> 168 us (0.960)
  Pallas kernels: 170 us -> 162 us
    pallas_call x2, Pallas kernels: 170 us -> 162 us  [the longest x1 159 us: exchange(): pl.pallas_call(exchange_kernel, out_shape=(pltpu.VMEM(factor_w.shape, f32...]
where the time goes in v3:
time: 168 us
  Pallas kernels  162 us (96%)
  local copies, waits for them, and re-layouts  2.63 us (2%)
  between operations  1.96 us (1%)
    pallas_call x1, Pallas kernels, exchange(): pl.pallas_call(exchange_kernel, out_shape=(pltpu.VMEM(factor_w.shape, f32...  159 us

profile of v3, /device:TPU:1, one launch (start us, length us, event | category | flops | bytes accessed | tf_op | source)
XLA Modules:
  0.0 167.6 jit_solution(3374036291459156572)
XLA Ops:
  0.6 0.7 reduce.2
  1.3 0.7 reshape.240.owner_ref.owner_item_ref
  2.0 1.4 reshape.241.local_ref.local_item_ref
  4.0 159.0 %shard_map.119 = (f32[3,1024,256]{2,1,0:T(8,128)S(1)}, f32[3,256,256]{2,1,0:T(8,128)}, f32[3,256]{1,0:T(4,128)}, f32[3,256]{1,0:T(4,128)}, s32[1]{0:T(128)}) custom-call(s32[16,96]{1,0:T(8,128)} %reshape.240.owner_ref.owner_item_ref, s32[16,96]{1,0:T(8,128)} %reshape.241.local_ref.local_item_ref, s32[16,96]{1,0:T(8,128)} %reshape.240.owner_ref.owner_item_ref, ...), custom_call_target="tpu_custom_call" | custom-call | tf_op jit(solution)/shard_map/pallas_call | solution.py:498
  163.7 3.1 %shard_map.120 = (f32[3,1024,256]{2,1,0:T(8,128)}, f32[3,256,256]{2,1,0:T(8,128)}, f32[3,256]{1,0:T(4,128)S(1)}, f32[3,256]{1,0:T(4,128)S(1)}) custom-call(f32[3,1024,256]{2,1,0:T(8,128)S(1)} %get-tuple-element.42.pj_ref, f32[3,256,256]{2,1,0:T(8,128)} %get-tuple-element.43.jj_ref, f32[3,256]{1,0:T(4,128)} %get-tuple-element.44.variance_ref, ...), custom_call_target="tpu_custom_call" | custom-call | tf_op jit(solution)/shard_map/pallas_call | solution.py:639
  166.8 0.2 conditional.1
  167.0 0.0 copy-start.5
  167.0 0.0 copy-start.6
  167.1 0.6 copy-done.5
  167.6 0.0 copy-done.6
Async XLA Ops:
  167.0 0.6 copy-start.5
  167.0 0.6 copy-start.6
